TPU v7x, 512 devices: a whole 4x4x16 slice. The times are simulated.
512 devices in a mesh: dp: 8 (over y, x_hi), ctx: 32 (over z, core), mp: 2 (over x_lo).
Axes of the slice: x: 4 (x_hi: 2, x_lo: 2; x = x_hi * 2 + x_lo), y: 4, z: 16, core: 2. Of those that a mesh axis runs over, the one named last changes fastest.
Arguments:
- query_input: bfloat16 [8, 14336, 1024], P('dp', 'ctx', 'mp'), may hold values from -6 to 6
- key_input: bfloat16 [8, 14336, 1024], P('dp', 'ctx', 'mp'), may hold values from -6 to 6
- value_input: bfloat16 [8, 14336, 1024], P('dp', 'ctx', 'mp'), may hold values from -6 to 6
- taps: float32 [3, 3, 1024], P(None, None, 'mp'), may hold values from -1.5 to 1.5
- grad_out: bfloat16 [8, 14336, 1024], P('dp', 'ctx', 'mp'), may hold values from -6 to 6
Outputs:
- attn_out: bfloat16 [8, 14336, 1024], P('dp', 'ctx', 'mp')
- grad_q: bfloat16 [8, 14336, 1024], P('dp', 'ctx', 'mp')
- grad_k: bfloat16 [8, 14336, 1024], P('dp', 'ctx', 'mp')
- value_input_gradient: bfloat16 [8, 14336, 1024], P('dp', 'ctx', 'mp')
- grad_taps: float32 [3, 3, 1024], P(None, None, 'mp')
All inputs are finite; a program needn't handle non-finite values.
Results may differ from a plain program's by a relative error of at most 0.0034.
The roundings to bfloat16 on the way count: a program that leaves them out, or rounds other values in their place, can miss the bound.
Values may be sent and summed in bfloat16 or wider, within the bound.
A program may use at most 64 MiB of HBM per device.

v0:
```python
import jax
import jax.numpy as jnp
from jax import lax
from jax.sharding import PartitionSpec as P

HEAD_DIM = 128
STEPS = 3


def from_behind(value, axis, steps):
    count = lax.axis_size(axis)
    pairs = [(source, (source + steps) % count) for source in range(count)]
    return lax.ppermute(value, axis, pairs)


def featurize(extended, tap, rows):
    total = jnp.zeros((rows, extended.shape[1]), jnp.float32)
    for j in range(3):
        total = total + tap[j] * extended[2 - j : 2 - j + rows].astype(jnp.float32)
    return total.astype(jnp.bfloat16)


def featurizer_adjoint(extended, tap, rows):
    total = jnp.zeros((rows, extended.shape[1]), jnp.float32)
    for j in range(3):
        total = total + tap[j] * extended[j : j + rows].astype(jnp.float32)
    return total.astype(jnp.bfloat16)


def head_major(flat, heads):
    return flat.reshape(flat.shape[0], heads, HEAD_DIM).transpose(1, 0, 2)


def head_scores(q_one, key_one, visible, scale):
    scores = jnp.einsum("qd,kd->qk", q_one, key_one, preferred_element_type=jnp.float32) * scale
    return jnp.where(visible, scores, -jnp.inf)


def shards(query_input, key_input, value_input, taps, grad_out):
    rows = query_input.shape[1]
    width = query_input.shape[2]
    heads = width // HEAD_DIM
    scale = HEAD_DIM ** (-0.5)
    raws = (query_input[0], key_input[0], value_input[0])
    edges = jnp.stack([unfiltered_input[rows - 2 :] for unfiltered_input in raws])
    rim = from_behind(edges, "ctx", 1)
    extended = [jnp.concatenate([rim[a], raws[a]], 0) for a in range(3)]
    qf = featurize(extended[0], taps[0], rows)
    kf = featurize(extended[1], taps[1], rows)
    vf = featurize(extended[2], taps[2], rows)
    key_parts, value_parts = ([kf], [vf])
    cur_k, cur_v = (kf, vf)
    for step in range(STEPS):
        cur_k, cur_v = from_behind((cur_k, cur_v), "ctx", 1)
        key_parts.append(cur_k)
        value_parts.append(cur_v)
    key_heads = head_major(jnp.concatenate(key_parts, 0), heads)
    value_heads = head_major(jnp.concatenate(value_parts, 0), heads)
    nkeys = key_heads.shape[1]
    row_pos = lax.broadcasted_iota(jnp.int32, (rows, nkeys), 0)
    col_pos = lax.broadcasted_iota(jnp.int32, (rows, nkeys), 1)
    visible = (col_pos >= rows) | (col_pos <= row_pos)
    q_heads = head_major(qf, heads)

    def forward_head(parts):
        q_one, key_one, value_one = parts
        scores = head_scores(q_one, key_one, visible, scale)
        peak = jnp.max(scores, axis=-1)
        total = jnp.sum(jnp.exp(scores - peak[:, None]), axis=-1)
        log_norm = peak + jnp.log(total)
        probs_b = jnp.exp(scores - log_norm[:, None]).astype(jnp.bfloat16)
        attended = jnp.einsum("qk,kd->qd", probs_b, value_one, preferred_element_type=jnp.float32)
        return (attended.astype(jnp.bfloat16), log_norm)

    attn_heads, norm_heads = lax.map(forward_head, (q_heads, key_heads, value_heads))
    attn_out = attn_heads.transpose(1, 0, 2).reshape(1, rows, width)
    key_parts, value_parts = ([kf], [vf])
    cur_k, cur_v = (kf, vf)
    for step in range(STEPS):
        cur_k, cur_v = from_behind((cur_k, cur_v), "ctx", 1)
        key_parts.append(cur_k)
        value_parts.append(cur_v)
    key_back = head_major(jnp.concatenate(key_parts, 0), heads)
    value_back = head_major(jnp.concatenate(value_parts, 0), heads)
    cotangent = head_major(grad_out[0], heads)

    def backward_head(parts):
        q_one, key_one, value_one, grad_one, log_norm = parts
        scores = head_scores(q_one, key_one, visible, scale)
        probs = jnp.exp(scores - log_norm[:, None])
        probs_b = probs.astype(jnp.bfloat16)
        prob_grad = jnp.einsum("qd,kd->qk", grad_one, value_one, preferred_element_type=jnp.float32)
        delta = jnp.sum(probs * prob_grad, axis=-1)
        score_grad = (probs * (prob_grad - delta[:, None])).astype(jnp.bfloat16)
        query_grad = scale * jnp.einsum(
            "qk,kd->qd", score_grad, key_one, preferred_element_type=jnp.float32
        )
        key_grad = scale * jnp.einsum(
            "qk,qd->kd", score_grad, q_one, preferred_element_type=jnp.float32
        )
        value_grad = jnp.einsum("qk,qd->kd", probs_b, grad_one, preferred_element_type=jnp.float32)
        return (query_grad, key_grad, value_grad)

    query_heads, key_grad_heads, value_grad_heads = lax.map(
        backward_head, (q_heads, key_back, value_back, cotangent, norm_heads)
    )
    dq_full = query_heads.transpose(1, 0, 2).reshape(rows, width)
    dk_terms = key_grad_heads.transpose(1, 0, 2).reshape(STEPS + 1, rows, width)
    dv_terms = value_grad_heads.transpose(1, 0, 2).reshape(STEPS + 1, rows, width)
    carry_k, carry_v = (dk_terms[0], dv_terms[0])
    for step in range(1, STEPS + 1):
        carry_k, carry_v = from_behind((carry_k, carry_v), "ctx", 1)
        carry_k = carry_k + dk_terms[step]
        carry_v = carry_v + dv_terms[step]
    dk_sum, dv_sum = (
        from_behind(carry_k.astype(jnp.bfloat16), "ctx", -STEPS).astype(carry_k.dtype),
        from_behind(carry_v.astype(jnp.bfloat16), "ctx", -STEPS).astype(carry_v.dtype),
    )
    dfeats = (
        dq_full.astype(jnp.bfloat16),
        dk_sum.astype(jnp.bfloat16),
        dv_sum.astype(jnp.bfloat16),
    )
    starts = jnp.stack([feature_gradient[:2] for feature_gradient in dfeats])
    tail = from_behind(starts, "ctx", -1)
    grads = []
    partial_rows = []
    for a in range(3):
        dext = jnp.concatenate([dfeats[a], tail[a]], 0)
        grads.append(featurizer_adjoint(dext, taps[a], rows).reshape(1, rows, width))
        dfloat = dfeats[a].astype(jnp.float32)
        partial_rows.append(
            jnp.stack(
                [
                    jnp.sum(dfloat * extended[a][2 - j : 2 - j + rows].astype(jnp.float32), axis=0)
                    for j in range(3)
                ]
            )
        )
    grad_taps = lax.psum(jnp.stack(partial_rows), ("dp", "ctx"))
    return (attn_out, grads[0], grads[1], grads[2], grad_taps)


def solution(mesh):
    return jax.shard_map(
        shards,
        mesh=mesh,
        in_specs=(
            P("dp", "ctx", "mp"),
            P("dp", "ctx", "mp"),
            P("dp", "ctx", "mp"),
            P(None, None, "mp"),
            P("dp", "ctx", "mp"),
        ),
        out_specs=(
            P("dp", "ctx", "mp"),
            P("dp", "ctx", "mp"),
            P("dp", "ctx", "mp"),
            P("dp", "ctx", "mp"),
            P(None, None, "mp"),
        ),
        check_vma=False,
    )
```

profile of v0, /device:TPU:2, one launch (start us, length us, event | category | flops | bytes accessed | tf_op | source)
XLA Modules:
  0.0 1506.8 jit_solution(4447731511729586331)
XLA Ops:
  3.7 9.4 collective-permute-done
  13.1 1.8 fusion.51
  14.9 1.8 fusion.48
  16.8 7.2 collective-permute-done.4
  24.0 4.9 collective-permute-done.1
  29.0 4.9 collective-permute-done.5
  35.3 3.6 collective-permute-done.2
  40.0 3.8 collective-permute-done.6
  43.8 1.8 bitcast_bitcast_fusion
  45.6 3.0 collective-permute-done.3
  48.6 2.6 bitcast_bitcast_fusion.1
  51.2 14.9 while.28
  55.0 1.8 fusion.101
  58.7 1.8 fusion.101
  66.2 47.7 %while.29 = (s32[]{:T(128)}, bf16[4,448,128]{2,0,1:T(4,128)(2,1)S(1)}, f32[4,1792,128]{2,1,0:T(8,128)}, f32[4,1792,128]{2,1,0:T(8,128)}, bf16[4,448,128]{2,1,0:T...) while((s32[]{:T(128)}, ...), condition=%wide.region_6.7_spmd.clone, body=%wide.region_4.6_spmd.clone.sunk | while | flops 1036721728 | bytes 37633208 | solution.py:104
  73.1 4.9 dynamic_update_slice.36
  85.1 4.9 dynamic_update_slice.36
  97.0 4.9 dynamic_update_slice.36
  109.0 4.9 dynamic_update_slice.36
  113.9 2.5 slice_bitcast_fusion.4
  117.5 13.0 collective-permute-done.7
  130.7 9.7 collective-permute-done.11
  140.5 9.7 collective-permute-done.8
  150.4 9.7 collective-permute-done.12
  160.2 9.6 collective-permute-done.9
  170.7 1.9 collective-permute-start.10
  172.6 7.0 collective-permute-done.13
  180.6 2.2 collective-permute-start.14
  183.2 8.5 collective-permute-done.10
  191.6 11.4 collective-permute-done.14
  207.6 3.3 fusion.55
  212.5 1293.3 %psum.7 = f32[3,3,512]{2,1,0:T(4,128)} all-reduce(f32[3,3,512]{2,1,0:T(4,128)S(1)} %pad_maximum_fusion.6), channel_id=1, replica_groups=mesh['dp'=8,'ctx'=32,'mp'=2] {'dp','ctx'}, use_global_device_ids=true, to_apply=%region_16.17 | all-reduce | flops 4608 | bytes 36864 | tf_op jit(solution)/shard_map/psum | solution.py:140
  (142 shorter events, 55.6 us)
Async XLA Ops:
  0.6 38.2 %copy-start.3 = (bf16[1,448,512]{2,1,0:T(8,128)(2,1)S(1)}, bf16[1,448,512]{2,1,0:T(8,128)(2,1)}, u32[]{:S(2)}) copy-start(bf16[1,448,512]{2,1,0:T(8,128)(2,1)} %param.9) | copy-start | bytes 1376260
  2.8 10.3 collective-permute-start
  14.9 14.1 copy-start.8
  14.9 9.1 collective-permute-start.4
  16.7 17.1 %copy-start.6 = (bf16[448,512]{1,0:T(8,128)(2,1)}, bf16[448,512]{1,0:T(8,128)(2,1)S(1)}, u32[]{:S(2)}) copy-start(bf16[448,512]{1,0:T(8,128)(2,1)S(1)} %fusion.48) | copy-start | bytes 1376260
  16.8 12.2 collective-permute-start.1
  24.0 4.9 copy-start.12
  24.0 9.8 collective-permute-start.5
  28.9 11.0 copy-start.10
  28.9 9.9 collective-permute-start.2
  33.8 6.1 copy-start.13
  33.9 9.9 collective-permute-start.6
  35.2 13.4 copy-start.7
  38.9 9.7 collective-permute-start.3
  43.8 4.8 copy-start.11
  66.2 1.6 copy-start.5
  78.1 1.6 copy-start.5
  90.0 1.6 copy-start.5
  101.9 1.6 copy-start.5
  113.9 3.1 copy-start.4
  116.5 14.0 collective-permute-start.7
  117.5 22.9 %collective-permute-start.11 = (f32[448,512]{1,0:T(8,128)S(1)}, f32[448,512]{1,0:T(8,128)S(1)}, u32[]{:S(2)}, u32[]{:S(2)}) collective-permute-start(f32[448,512]{1,0:T(8,128)S(1)} %bitcast.229), channel_id=1, source_target_pairs={{0,2},{2,4},{4,6},{6,8},{8,10},{10,12},{12,14},{14,16},{16,18},{18... | collective-permute-start | bytes 2752520 | tf_op jit(solution)/shard_map/ppermute | solution.py:13
  130.7 19.5 %collective-permute-start.8 = (f32[448,512]{1,0:T(8,128)S(1)}, f32[448,512]{1,0:T(8,128)S(1)}, u32[]{:S(2)}, u32[]{:S(2)}) collective-permute-start(f32[448,512]{1,0:T(8,128)S(1)} %bitcast_add_fusion.5), channel_id=1, source_target_pairs={{0,2},{2,4},{4,6},{6,8},{8,10},{10,12},{12,14},{14,16},{16,18},{18... | collective-permute-start | bytes 2752520 | tf_op jit(solution)/shard_map/ppermute | solution.py:13
  140.5 19.5 %collective-permute-start.12 = (f32[448,512]{1,0:T(8,128)S(1)}, f32[448,512]{1,0:T(8,128)S(1)}, u32[]{:S(2)}, u32[]{:S(2)}) collective-permute-start(f32[448,512]{1,0:T(8,128)S(1)} %bitcast_add_fusion.2), channel_id=1, source_target_pairs={{0,2},{2,4},{4,6},{6,8},{8,10},{10,12},{12,14},{14,16},{16,18},{18... | collective-permute-start | bytes 2752520 | tf_op jit(solution)/shard_map/ppermute | solution.py:13
  150.3 19.5 %collective-permute-start.9 = (f32[448,512]{1,0:T(8,128)S(1)}, f32[448,512]{1,0:T(8,128)S(1)}, u32[]{:S(2)}, u32[]{:S(2)}) collective-permute-start(f32[448,512]{1,0:T(8,128)S(1)} %bitcast_add_fusion.4), channel_id=1, source_target_pairs={{0,2},{2,4},{4,6},{6,8},{8,10},{10,12},{12,14},{14,16},{16,18},{18... | collective-permute-start | bytes 2752520 | tf_op jit(solution)/shard_map/ppermute | solution.py:13
  160.2 19.5 %collective-permute-start.13 = (f32[448,512]{1,0:T(8,128)S(1)}, f32[448,512]{1,0:T(8,128)S(1)}, u32[]{:S(2)}, u32[]{:S(2)}) collective-permute-start(f32[448,512]{1,0:T(8,128)S(1)} %bitcast_add_fusion.1), channel_id=1, source_target_pairs={{0,2},{2,4},{4,6},{6,8},{8,10},{10,12},{12,14},{14,16},{16,18},{18... | collective-permute-start | bytes 2752520 | tf_op jit(solution)/shard_map/ppermute | solution.py:13
  170.7 20.9 %collective-permute-start.10 = (bf16[448,512]{1,0:T(8,128)(2,1)}, bf16[448,512]{1,0:T(8,128)(2,1)S(1)}, u32[]{:S(2)}, u32[]{:S(2)}) collective-permute-start(bf16[448,512]{1,0:T(8,128)(2,1)} %fusion.70), channel_id=1, source_target_pairs={{0,58},{2,60},{4,62},{6,0},{8,2},{10,4},{12,6},{14,8},{16,10},{18,... | collective-permute-start | bytes 1376264 | tf_op jit(solution)/shard_map/ppermute | solution.py:13
  180.6 27.0 %copy-start.1 = (bf16[1,448,512]{2,1,0:T(8,128)(2,1)S(1)}, bf16[1,448,512]{2,1,0:T(8,128)(2,1)}, u32[]{:S(2)}) copy-start(bf16[1,448,512]{2,1,0:T(8,128)(2,1)} %param.10) | copy-start | bytes 1376260
  180.6 22.5 %collective-permute-start.14 = (bf16[448,512]{1,0:T(8,128)(2,1)}, bf16[448,512]{1,0:T(8,128)(2,1)S(1)}, u32[]{:S(2)}, u32[]{:S(2)}) collective-permute-start(bf16[448,512]{1,0:T(8,128)(2,1)} %fusion.69), channel_id=1, source_target_pairs={{0,58},{2,60},{4,62},{6,0},{8,2},{10,4},{12,6},{14,8},{16,10},{18,... | collective-permute-start | bytes 1376264 | tf_op jit(solution)/shard_map/ppermute | solution.py:13
  191.6 11.5 copy-start.9
  203.1 7.9 copy-start.2
  203.1 4.5 collective-permute-start.15
  (4 other events, 6.0 us)
where the time goes:
time: 1510 us
  blocking collectives  1290 us (85%)
  waiting for transfers between devices  115 us (8%)
  matrix products  35 us (2%)
  local copies, waits for them, and re-layouts  34.3 us (2%)
  other arithmetic  21.6 us (1%)
    psum x1, blocking collectives, shards(): grad_taps = lax.psum(jnp.stack(partial_rows), ('dp', 'ctx'))  1290 us
    ppermute x16, waiting for transfers between devices, from_behind(): return lax.ppermute(value, axis, pairs)  115 us
  transfers between devices with their start and end apart: 16, of which 15 were waited for; matrix products, arithmetic and copies ran while one was open for 1% of the time, Pallas kernels for 0%

commit v1 on v0

v1 whole, which is shorter than its diff:
```python
import functools

import jax
import jax.numpy as jnp
from jax import lax
from jax.experimental import pallas as pl
from jax.experimental.pallas import tpu as pltpu
from jax.sharding import PartitionSpec as P

HEAD_DIM = 128
STEPS = 3
BLOCKS = STEPS + 1
RIM = 16
MESH = pl.DeviceIdType.MESH
BF16 = jnp.bfloat16
F32 = jnp.float32
NT = (((1,), (1,)), ((), ()))
NN = (((1,), (0,)), ((), ()))
TN = (((0,), (0,)), ((), ()))


def dot(a, b, dims):
    return lax.dot_general(a, b, dims, preferred_element_type=F32)


def reduction_rounds(dp, ctx):
    if (dp, ctx) == (8, 32):
        return (
            (("ctx", 1, 2), ("dp", 1, 2)),
            (("dp", 2, 4),),
            (("ctx", 2, 4),),
            (("ctx", 8, 4),),
        )
    return tuple(((name, 1, size),) for name, size in (("dp", dp), ("ctx", ctx)) if size > 1)


class Group:
    def __init__(self, digits, place):
        self.digits = digits
        self.place = place
        self.size = 1
        self.index = 0
        for name, stride, size in digits:
            self.index = self.index * size + (place[name] // stride) % size
            self.size *= size

    def other(self, ahead):
        slot = lax.rem(self.index + ahead, self.size)
        rest = slot
        device = {}
        for name, stride, size in reversed(self.digits):
            digit = lax.rem(rest, size)
            rest = rest // size
            mine = (self.place[name] // stride) % size
            device[name] = self.place[name] + (digit - mine) * stride
        return slot, device


def kernel(
    sizes, q_hbm, k_hbm, v_hbm, taps_ref, g_hbm,
    out_hbm, gq_hbm, gk_hbm, gv_hbm, gt_ref,
    raw, qraw, gbuf, ext, qext, kfb, vfb, qfb, pbuf, dsbuf, dkv, dqb,
    rf32, rb16, sb16, tail_out, tail_in, dext, obuf, abuf, total, slots,
    in_sem, out_sem, attn_sem, rim_send, rim_recv, fwd_send, fwd_recv, bwd_send, bwd_recv,
    tail_send, tail_recv, sum_send, sum_recv,
):
    rows, heads, n_dp, n_ctx = sizes
    nkeys = BLOCKS * rows
    split = (nkeys - rows) // 128 * 128
    offset = nkeys - rows - split
    tile = rows // 2
    chunk = rows // 4
    scale = HEAD_DIM ** (-0.5)
    exp_scale = scale * 1.4426950408889634

    me = lax.axis_index("ctx")
    place = {"ctx": me, "dp": lax.axis_index("dp")}
    core = lax.rem(me, 2)
    ahead = {"ctx": lax.rem(me + 1, n_ctx)}
    behind = {"ctx": lax.rem(me + n_ctx - 1, n_ctx)}
    far_ahead = {"ctx": lax.rem(me + BLOCKS, n_ctx)}
    far_behind = {"ctx": lax.rem(me + n_ctx - BLOCKS, n_ctx)}
    groups = [Group(digits, place) for digits in reduction_rounds(n_dp, n_ctx)]

    def columns(h):
        return pl.ds(h * HEAD_DIM, HEAD_DIM)

    def load(h, n):
        source = (k_hbm, v_hbm, q_hbm, g_hbm)[n].at[:, columns(h)]
        if n < 2:
            target = raw.at[h, n, pl.ds(RIM + STEPS * rows, rows), :]
        elif n == 2:
            target = qraw.at[h, pl.ds(RIM, rows), :]
        else:
            target = gbuf.at[h]
        return pltpu.make_async_copy(source, target, in_sem.at[h, n])

    for h in range(heads):
        for n in range(4):
            load(h, n).start()

    barrier = pltpu.get_barrier_semaphore()
    partners = [ahead, behind, far_ahead, far_behind]
    for group in groups:
        for m in range(1, group.size):
            partners.append(group.other(m)[1])
    for partner in partners:
        pl.semaphore_signal(barrier, inc=1, device_id=partner, device_id_type=MESH)
    pl.semaphore_wait(barrier, len(partners))

    for h in range(heads):
        for n in range(4):
            load(h, n).wait()

    def pass_on(step, h, a):
        return pltpu.make_async_remote_copy(
            src_ref=raw.at[h, a, pl.ds(RIM + (STEPS - step) * rows, rows), :],
            dst_ref=raw.at[h, a, pl.ds(RIM + (STEPS - 1 - step) * rows, rows), :],
            send_sem=fwd_send.at[step, h, a],
            recv_sem=fwd_recv.at[step, h, a],
            device_id=ahead,
            device_id_type=MESH,
        )

    def send_step(step, h):
        for a in range(2):
            if step > 0:
                pass_on(step - 1, h, a).wait_recv()
            pass_on(step, h, a).start()

    q_rim = pltpu.make_async_remote_copy(
        src_ref=qraw.at[:, pl.ds(rows, RIM), :],
        dst_ref=qraw.at[:, pl.ds(0, RIM), :],
        send_sem=rim_send.at[0],
        recv_sem=rim_recv.at[0],
        device_id=ahead,
        device_id_type=MESH,
    )
    kv_rim = pltpu.make_async_remote_copy(
        src_ref=raw.at[:, :, pl.ds(nkeys, RIM), :],
        dst_ref=raw.at[:, :, pl.ds(0, RIM), :],
        send_sem=rim_send.at[1],
        recv_sem=rim_recv.at[1],
        device_id=far_ahead,
        device_id_type=MESH,
    )

    send_step(0, 0)
    q_rim.start()
    kv_rim.start()
    total[...] = jnp.zeros_like(total)
    send_step(1, 0)
    send_step(2, 0)
    if heads > 1:
        send_step(0, 1)
    q_rim.wait_recv()
    kv_rim.wait_recv()

    def bwd_narrow(step, h, a):
        return pltpu.make_async_remote_copy(
            src_ref=sb16.at[h, step, a],
            dst_ref=rb16.at[h, step, a],
            send_sem=bwd_send.at[step, h, a],
            recv_sem=bwd_recv.at[step, h, a],
            device_id=behind,
            device_id_type=MESH,
        )

    def bwd_wide(step, h, a):
        return pltpu.make_async_remote_copy(
            src_ref=dkv.at[h, a, pl.ds(step * rows, rows), :],
            dst_ref=rf32.at[h, step, a],
            send_sem=bwd_send.at[step, h, a],
            recv_sem=bwd_recv.at[step, h, a],
            device_id=behind,
            device_id_type=MESH,
        )

    def send_back(step, h):
        @pl.when(core == 0)
        def _():
            for a in range(2):
                if step > 0:
                    bwd_wide(step - 1, h, a).wait_recv()

                def piece(i, carry):
                    at = pl.multiple_of(i * chunk, 16)
                    term = dkv[h, a, pl.ds(step * rows + at, chunk), :]
                    if step > 0:
                        term = term + rf32[h, step - 1, a, pl.ds(at, chunk), :]
                    sb16[h, step, a, pl.ds(at, chunk), :] = term.astype(BF16)
                    return carry

                lax.fori_loop(0, rows // chunk, piece, 0)
                bwd_narrow(step, h, a).start()

        @pl.when(core == 1)
        def _():
            for a in range(2):
                if step > 0:
                    bwd_narrow(step - 1, h, a).wait_recv()

                    def piece(i, carry):
                        at = pl.multiple_of(i * chunk, 16)
                        here = pl.ds(step * rows + at, chunk)
                        came = rb16[h, step - 1, a, pl.ds(at, chunk), :].astype(F32)
                        dkv[h, a, here, :] = dkv[h, a, here, :] + came
                        return carry

                    lax.fori_loop(0, rows // chunk, piece, 0)
                bwd_wide(step, h, a).start()

    def tail(h):
        return pltpu.make_async_remote_copy(
            src_ref=tail_out.at[h],
            dst_ref=tail_in.at[h],
            send_sem=tail_send.at[h],
            recv_sem=tail_recv.at[h],
            device_id=behind,
            device_id_type=MESH,
        )

    def settle(h):
        last = STEPS - 1

        @pl.when(core == 0)
        def _():
            for a in range(2):
                bwd_wide(last, h, a).wait_recv()

        @pl.when(core == 1)
        def _():
            for a in range(2):
                bwd_narrow(last, h, a).wait_recv()

        def piece(i, carry):
            at = pl.multiple_of(i * chunk, 16)
            here = pl.ds(at, chunk)
            dext[0, here, :] = dqb[h, here, :].astype(F32)
            for a in range(2):
                own = dkv[h, a, pl.ds(STEPS * rows + at, chunk), :]

                @pl.when(core == 0)
                def _():
                    dext[a + 1, here, :] = (own + rf32[h, last, a, here, :]).astype(BF16).astype(F32)

                @pl.when(core == 1)
                def _():
                    came = rb16[h, last, a, here, :].astype(F32)
                    dext[a + 1, here, :] = (own + came).astype(BF16).astype(F32)

            return carry

        lax.fori_loop(0, rows // chunk, piece, 0)
        for a in range(3):
            tail_out[h, a] = dext[a, pl.ds(0, RIM), :].astype(BF16)
        tail(h).start()

    def tap(a, j, h):
        return taps_ref[a, pl.ds(j, 1), columns(h)]

    def store(h, a):
        target = (gq_hbm, gk_hbm, gv_hbm)[a]
        return pltpu.make_async_copy(obuf.at[h, a], target.at[:, columns(h)], out_sem.at[h, a])

    def finish(h):
        tail(h).wait_recv()
        for a in range(3):
            dext[a, pl.ds(rows, RIM), :] = tail_in[h, a].astype(F32)
            taps_here = [tap(a, j, h) for j in range(3)]
            for i in range(rows // chunk):
                value = jnp.zeros((chunk, HEAD_DIM), F32)
                for j in range(3):
                    value = value + taps_here[j] * dext[a, pl.ds(i * chunk + j, chunk), :]
                obuf[h, a, pl.ds(i * chunk, chunk), :] = value.astype(BF16)
            store(h, a).start()

    def featurize(h):
        for a, (source, wide, target, blocks) in enumerate(
            (
                (qraw.at[h], qext, qfb, 1),
                (raw.at[h, 0], ext.at[0], kfb, BLOCKS),
                (raw.at[h, 1], ext.at[1], vfb, BLOCKS),
            )
        ):
            taps_here = [tap(a, j, h) for j in range(3)]
            wide[pl.ds(0, RIM), :] = source[pl.ds(0, RIM), :].astype(F32)
            for i in range(blocks * rows // chunk):
                here = pl.ds(RIM + i * chunk, chunk)
                wide[here, :] = source[here, :].astype(F32)
                value = jnp.zeros((chunk, HEAD_DIM), F32)
                for j in range(3):
                    value = value + taps_here[j] * wide[pl.ds(RIM + i * chunk - j, chunk), :]
                target[pl.ds(i * chunk, chunk), :] = value.astype(BF16)

    def attend(h, i):
        here = pl.ds(i * tile, tile)
        q = qfb[here, :]
        g = gbuf[h, here, :]
        parts = (pl.ds(0, split), pl.ds(split, nkeys - split))
        scores = [dot(q, kfb[part, :], NT) for part in parts]
        row = lax.broadcasted_iota(jnp.int32, scores[1].shape, 0) + i * tile
        col = lax.broadcasted_iota(jnp.int32, scores[1].shape, 1) - offset
        scores[1] = jnp.where(col <= row, scores[1], -jnp.inf)
        peak = jnp.maximum(
            jnp.max(scores[0], axis=1, keepdims=True), jnp.max(scores[1], axis=1, keepdims=True)
        )
        weights = [jnp.exp2((score - peak) * exp_scale) for score in scores]
        norm = jnp.sum(weights[0], axis=1, keepdims=True) + jnp.sum(weights[1], axis=1, keepdims=True)
        inverse = 1.0 / norm
        probs = [weight * inverse for weight in weights]
        attended = jnp.zeros((tile, HEAD_DIM), F32)
        for part, prob in zip(parts, probs, strict=True):
            prob_b = prob.astype(BF16)
            pbuf[here, part] = prob_b
            attended = attended + dot(prob_b, vfb[part, :], NN)
        abuf[h, here, :] = attended.astype(BF16)
        terms = [prob * dot(g, vfb[part, :], NT) for part, prob in zip(parts, probs, strict=True)]
        delta = jnp.sum(terms[0], axis=1, keepdims=True) + jnp.sum(terms[1], axis=1, keepdims=True)
        query_grad = jnp.zeros((tile, HEAD_DIM), F32)
        for part, prob, term in zip(parts, probs, terms, strict=True):
            score_grad = (term - prob * delta).astype(BF16)
            dsbuf[here, part] = score_grad
            query_grad = query_grad + dot(score_grad, kfb[part, :], NN)
        dqb[h, here, :] = (query_grad * scale).astype(BF16)

    def attn_store(h):
        return pltpu.make_async_copy(abuf.at[h], out_hbm.at[:, columns(h)], attn_sem.at[h])

    def key_gradients(h):
        attn_store(h).start()
        dkv[h, 0] = (dot(qfb[...], dsbuf[...], TN) * scale).T
        dkv[h, 1] = dot(gbuf[h], pbuf[...], TN).T
        send_back(0, h)

        def piece(i, carry):
            at = pl.multiple_of(i * chunk, 16)
            sums = list(carry)
            for a in range(2):
                term = dkv[h, a, pl.ds(at, chunk), :]
                for j in range(3):
                    near = ext[a, pl.ds(RIM - j + at, chunk), :]
                    sums[a * 3 + j] = sums[a * 3 + j] + jnp.sum(
                        (term * near).reshape(chunk // 8, 8, HEAD_DIM), axis=0
                    )
            return tuple(sums)

        sums = lax.fori_loop(
            0, nkeys // chunk, piece, tuple(jnp.zeros((8, HEAD_DIM), F32) for _ in range(6))
        )
        for j in range(3):
            query_sum = jnp.sum(
                dqb[h].astype(F32) * qext[pl.ds(RIM - j, rows), :], axis=0, keepdims=True
            )
            total[h, pl.ds(j, 1), :] = query_sum
        for n in range(6):
            total[h, pl.ds(3 + n, 1), :] = jnp.sum(sums[n], axis=0, keepdims=True)

    def head_step(h, carry):
        for a in range(2):
            pass_on(STEPS - 1, h, a).wait_recv()
        featurize(h)

        @pl.when(h < heads - 1)
        def _():
            send_step(1, h + 1)

        @pl.when(h > 1)
        def _():
            settle(h - 2)

        attend(h, 0)

        @pl.when(h < heads - 1)
        def _():
            send_step(2, h + 1)

        @pl.when(h < heads - 2)
        def _():
            send_step(0, h + 2)

        @pl.when(h > 0)
        def _():
            send_back(1, h - 1)

        @pl.when(h > 1)
        def _():
            finish(h - 2)

        attend(h, 1)

        @pl.when(h > 0)
        def _():
            send_back(2, h - 1)

        key_gradients(h)
        return carry

    lax.fori_loop(0, heads, head_step, 0)

    def sum_copy(n, m):
        group = groups[n]
        slot, device = group.other(m)
        return slot, pltpu.make_async_remote_copy(
            src_ref=slots.at[n, group.index],
            dst_ref=slots.at[n, group.index],
            send_sem=sum_send.at[n, m],
            recv_sem=sum_recv.at[n, group.index],
            device_id=device,
            device_id_type=MESH,
        )

    def sum_start(n, value):
        slots[n, groups[n].index] = value
        for m in range(1, groups[n].size):
            sum_copy(n, m)[1].start()

    def sum_end(n):
        group = groups[n]
        for m in range(1, group.size):
            slot, _ = group.other(m)
            pltpu.make_async_remote_copy(
                src_ref=slots.at[n, slot],
                dst_ref=slots.at[n, slot],
                send_sem=sum_send.at[n, m],
                recv_sem=sum_recv.at[n, slot],
                device_id=ahead,
                device_id_type=MESH,
            ).wait_recv()
        value = slots[n, 0]
        for slot in range(1, group.size):
            value = value + slots[n, slot]
        return value

    steps = []
    if heads > 1:
        steps.append(lambda: settle(heads - 2))
        steps.append(lambda: finish(heads - 2))
    steps.append(lambda: send_back(1, heads - 1))
    steps.append(lambda: send_back(2, heads - 1))
    steps.append(lambda: settle(heads - 1))
    steps.append(lambda: finish(heads - 1))

    sum_start(0, total[...])
    done = 0
    for n, step in enumerate(steps):
        step()
        if n > 0 and done < len(groups) - 1:
            sum_start(done + 1, sum_end(done))
            done += 1
    while done < len(groups) - 1:
        sum_start(done + 1, sum_end(done))
        done += 1
    value = sum_end(done)
    for h in range(heads):
        for a in range(3):
            gt_ref[a, :, columns(h)] = value[h, 3 * a : 3 * a + 3, :]

    for h in range(heads):
        attn_store(h).wait()
        tail(h).wait_send()
        for a in range(3):
            store(h, a).wait()
        for step in range(STEPS):
            for a in range(2):
                pass_on(step, h, a).wait_send()

    @pl.when(core == 0)
    def _():
        for h in range(heads):
            for step in range(STEPS):
                for a in range(2):
                    bwd_narrow(step, h, a).wait_send()

    @pl.when(core == 1)
    def _():
        for h in range(heads):
            for step in range(STEPS):
                for a in range(2):
                    bwd_wide(step, h, a).wait_send()

    q_rim.wait_send()
    kv_rim.wait_send()
    for n, group in enumerate(groups):
        for m in range(1, group.size):
            sum_copy(n, m)[1].wait_send()


def shards(n_dp, n_ctx, query_input, key_input, value_input, taps, grad_out):
    rows, width = query_input.shape[1:]
    heads = width // HEAD_DIM
    nkeys = BLOCKS * rows
    rounds = len(reduction_rounds(n_dp, n_ctx))
    members = 4 if (n_dp, n_ctx) == (8, 32) else max(n_dp, n_ctx)
    hbm = pl.BlockSpec(memory_space=pl.ANY)
    vmem = pl.BlockSpec(memory_space=pltpu.VMEM)
    flat = jax.ShapeDtypeStruct((rows, width), BF16)
    dma = pltpu.SemaphoreType.DMA
    block = (rows, HEAD_DIM)
    results = pl.pallas_call(
        functools.partial(kernel, (rows, heads, n_dp, n_ctx)),
        out_shape=(flat, flat, flat, flat, jax.ShapeDtypeStruct(taps.shape, F32)),
        in_specs=[hbm, hbm, hbm, vmem, hbm],
        out_specs=(hbm, hbm, hbm, hbm, vmem),
        scratch_shapes=[
            pltpu.VMEM((heads, 2, RIM + nkeys, HEAD_DIM), BF16),
            pltpu.VMEM((heads, RIM + rows, HEAD_DIM), BF16),
            pltpu.VMEM((heads, *block), BF16),
            pltpu.VMEM((2, RIM + nkeys, HEAD_DIM), F32),
            pltpu.VMEM((RIM + rows, HEAD_DIM), F32),
            pltpu.VMEM((nkeys, HEAD_DIM), BF16),
            pltpu.VMEM((nkeys, HEAD_DIM), BF16),
            pltpu.VMEM(block, BF16),
            pltpu.VMEM((rows, nkeys), BF16),
            pltpu.VMEM((rows, nkeys), BF16),
            pltpu.VMEM((heads, 2, nkeys, HEAD_DIM), F32),
            pltpu.VMEM((heads, *block), BF16),
            pltpu.VMEM((heads, STEPS, 2, *block), F32),
            pltpu.VMEM((heads, STEPS, 2, *block), BF16),
            pltpu.VMEM((heads, STEPS, 2, *block), BF16),
            pltpu.VMEM((heads, 3, RIM, HEAD_DIM), BF16),
            pltpu.VMEM((heads, 3, RIM, HEAD_DIM), BF16),
            pltpu.VMEM((3, rows + RIM, HEAD_DIM), F32),
            pltpu.VMEM((heads, 3, *block), BF16),
            pltpu.VMEM((heads, *block), BF16),
            pltpu.VMEM((heads, 16, HEAD_DIM), F32),
            pltpu.VMEM((rounds, members, heads, 16, HEAD_DIM), F32),
            dma((heads, 4)),
            dma((heads, 3)),
            dma((heads,)),
            dma((2,)),
            dma((2,)),
            dma((STEPS, heads, 2)),
            dma((STEPS, heads, 2)),
            dma((STEPS, heads, 2)),
            dma((STEPS, heads, 2)),
            dma((heads,)),
            dma((heads,)),
            dma((rounds, members)),
            dma((rounds, members)),
        ],
        compiler_params=pltpu.CompilerParams(
            collective_id=0, has_side_effects=True, vmem_limit_bytes=58 * 1024 * 1024
        ),
    )(query_input[0], key_input[0], value_input[0], taps, grad_out[0])
    return (*[result[None] for result in results[:4]], results[4])


def solution(mesh):
    sharded = P("dp", "ctx", "mp")
    return jax.shard_map(
        functools.partial(shards, mesh.shape["dp"], mesh.shape["ctx"]),
        mesh=mesh,
        in_specs=(sharded, sharded, sharded, P(None, None, "mp"), sharded),
        out_specs=(sharded, sharded, sharded, sharded, P(None, None, "mp")),
        check_vma=False,
    )
```

time: 1510 us -> 96.9 us (0.06)
  the two profiles are of different devices: /device:TPU:2 before, /device:TPU:32 now
where the time goes in v1:
time: 96.9 us; the launch traced here: 96.5 us
  Pallas kernels  90.3 us (93%)
  local copies, waits for them, and re-layouts  5.62 us (6%)
    pallas_call x1, Pallas kernels, shards(): pl.pallas_call(functools.partial(kernel, (rows, heads, n_dp, n_ctx)), out...  90.3 us
    unnamed x13, local copies, waits for them, and re-layouts  5.62 us

profile of v1, /device:TPU:32, one launch (start us, length us, event | category | flops | bytes accessed | tf_op | source)
XLA Modules:
  0.0 96.5 jit_solution(16539301063608842373)
XLA Ops:
  0.6 90.3 %shard_map.92 = (bf16[448,512]{1,0:T(8,128)(2,1)}, bf16[448,512]{1,0:T(8,128)(2,1)}, bf16[448,512]{1,0:T(8,128)(2,1)}, bf16[448,512]{1,0:T(8,128)(2,1)}, f32[3,3,512]{2,1,0:T(4,128)}) custom-call(bf16[448,512]{1,0:T(8,128)(2,1)} %bitcast.8, bf16[448,512]{1,0:T(8,128)(2,1)} %bitcast.9, bf16[448,512]{1,0:T(8,128)(2,1)} %bitcast.10, f32[3,3,512]{2,1,0:T(4,128)} %taps_ref.1, ...), custom_call_target="tpu_custom_call" | custom-call | tf_op jit(solution)/shard_map/pallas_call | solution.py:500
  90.9 0.0 copy-start.2
  90.9 1.9 %copy.15 = bf16[1,448,512]{2,1,0:T(8,128)(2,1)} copy(bf16[1,448,512]{2,1,0:T(8,128)(2,1)} %bitcast.15) | data formatting | bytes 917504
  92.8 0.0 copy-done.2
  92.8 0.0 copy-start.1
  92.8 0.8 copy.16
  93.6 0.4 copy-done.1
  94.0 0.0 copy-start
  94.0 0.8 copy.17
  94.7 0.4 copy-done
  95.2 0.0 copy-start.3
  95.2 0.8 copy.18
  95.9 0.0 copy-done.3
  95.9 0.6 copy.19
Async XLA Ops:
  90.9 1.9 %copy-start.2 = (bf16[448,512]{1,0:T(8,128)(2,1)S(1)}, bf16[448,512]{1,0:T(8,128)(2,1)}, u32[]{:S(2)}) copy-start(bf16[448,512]{1,0:T(8,128)(2,1)} %get-tuple-element.11) | copy-start | bytes 1376260
  92.8 1.2 %copy-start.1 = (bf16[448,512]{1,0:T(8,128)(2,1)S(1)}, bf16[448,512]{1,0:T(8,128)(2,1)}, u32[]{:S(2)}) copy-start(bf16[448,512]{1,0:T(8,128)(2,1)} %get-tuple-element.12) | copy-start | bytes 1376260
  94.0 1.2 %copy-start = (bf16[448,512]{1,0:T(8,128)(2,1)S(1)}, bf16[448,512]{1,0:T(8,128)(2,1)}, u32[]{:S(2)}) copy-start(bf16[448,512]{1,0:T(8,128)(2,1)} %get-tuple-element.13) | copy-start | bytes 1376260
  95.2 0.8 copy-start.3

commit v2 on v1

v2 whole, which is shorter than its diff:
```python
import functools

import jax
import jax.numpy as jnp
from jax import lax
from jax.experimental import pallas as pl
from jax.experimental.pallas import tpu as pltpu
from jax.sharding import PartitionSpec as P

HEAD_DIM = 128
STEPS = 3
BLOCKS = STEPS + 1
RIM = 16
MESH = pl.DeviceIdType.MESH
BF16 = jnp.bfloat16
F32 = jnp.float32
NT = (((1,), (1,)), ((), ()))
NN = (((1,), (0,)), ((), ()))
TN = (((0,), (0,)), ((), ()))


def dot(a, b, dims):
    return lax.dot_general(a, b, dims, preferred_element_type=F32)


def encode(value):
    return (value * jnp.abs(value)).astype(BF16)


def decode(code):
    code = code.astype(F32)
    return code * lax.rsqrt(jnp.maximum(jnp.abs(code), 1e-37))


def reduction_rounds(dp, ctx):
    if (dp, ctx) == (8, 32):
        return (
            (("ctx", 1, 2), ("dp", 1, 2)),
            (("dp", 2, 4),),
            (("ctx", 2, 4),),
            (("ctx", 8, 4),),
        )
    return tuple(((name, 1, size),) for name, size in (("dp", dp), ("ctx", ctx)) if size > 1)


class Group:
    def __init__(self, digits, place):
        self.digits = digits
        self.place = place
        self.size = 1
        self.index = 0
        for name, stride, size in digits:
            self.index = self.index * size + (place[name] // stride) % size
            self.size *= size

    def other(self, ahead):
        slot = lax.rem(self.index + ahead, self.size)
        rest = slot
        device = {}
        for name, stride, size in reversed(self.digits):
            digit = lax.rem(rest, size)
            rest = rest // size
            mine = (self.place[name] // stride) % size
            device[name] = self.place[name] + (digit - mine) * stride
        return slot, device


def kernel(
    sizes, q_hbm, k_hbm, v_hbm, taps_ref, g_hbm,
    out_ref, gq_ref, gk_ref, gv_ref, gt_ref,
    held, mine, rim_out, near_rim, far_rim, raw, wide_own, ext, norms, kfb, vfb, qfb, sbuf, dpbuf, pbuf, dsbuf, dkv, dqb,
    term_in, term_out, tail_out, tail_in, dext, total, slots,
    in_sem, rim_send, rim_recv, fwd_send, fwd_recv, bwd_send, bwd_recv,
    tail_send, tail_recv, sum_send, sum_recv,
):
    rows, heads, n_dp, n_ctx = sizes
    nkeys = BLOCKS * rows
    past = STEPS * rows
    tile = rows // 2
    strip = min(32, tile)
    chunk = rows // 4
    scale = HEAD_DIM ** (-0.5)
    exp_scale = scale * 1.4426950408889634

    me = lax.axis_index("ctx")
    place = {"ctx": me, "dp": lax.axis_index("dp")}
    ahead = {"ctx": lax.rem(me + 1, n_ctx)}
    behind = {"ctx": lax.rem(me + n_ctx - 1, n_ctx)}
    far_ahead = {"ctx": lax.rem(me + BLOCKS, n_ctx)}
    far_behind = {"ctx": lax.rem(me + n_ctx - BLOCKS, n_ctx)}

    def width_of(i):
        return -(-(past + (i + 1) * tile) // HEAD_DIM) * HEAD_DIM

    groups = [Group(digits, place) for digits in reduction_rounds(n_dp, n_ctx)]

    def columns(h):
        return pl.ds(pl.multiple_of(h * HEAD_DIM, HEAD_DIM), HEAD_DIM)

    def load(n):
        return pltpu.make_async_copy((q_hbm, k_hbm, v_hbm, g_hbm)[n], held.at[n], in_sem.at[n])

    for n in (1, 2, 0, 3):
        load(n).start()

    barrier = pltpu.get_barrier_semaphore()
    partners = [ahead, behind, far_ahead, far_behind]
    for group in groups:
        for m in range(1, group.size):
            partners.append(group.other(m)[1])
    for partner in partners:
        pl.semaphore_signal(barrier, inc=1, device_id=partner, device_id_type=MESH)
    pl.semaphore_wait(barrier, len(partners))

    def split(h, a):
        def piece(i, carry):
            here = pl.ds(pl.multiple_of(i * chunk, 16), chunk)
            mine[h, a, here, :] = held[a + 1, here, columns(h)]
            return carry

        lax.fori_loop(0, rows // chunk, piece, 0)

    def pass_on(step, h, a):
        here = pl.ds((STEPS - step) * rows, rows)
        return pltpu.make_async_remote_copy(
            src_ref=mine.at[h, a] if step == 0 else raw.at[h, a, here, :],
            dst_ref=raw.at[h, a, pl.ds((STEPS - 1 - step) * rows, rows), :],
            send_sem=fwd_send.at[step, h, a],
            recv_sem=fwd_recv.at[step, h, a],
            device_id=ahead,
            device_id_type=MESH,
        )

    def send_step(step, h):
        for a in range(2):
            if step > 0:
                pass_on(step - 1, h, a).wait_recv()
            else:
                split(h, a)
            pass_on(step, h, a).start()

    to_next = pltpu.make_async_remote_copy(
        src_ref=rim_out,
        dst_ref=near_rim,
        send_sem=rim_send.at[0],
        recv_sem=rim_recv.at[0],
        device_id=ahead,
        device_id_type=MESH,
    )
    to_far = pltpu.make_async_remote_copy(
        src_ref=rim_out.at[pl.ds(1, 2)],
        dst_ref=far_rim,
        send_sem=rim_send.at[1],
        recv_sem=rim_recv.at[1],
        device_id=far_ahead,
        device_id_type=MESH,
    )

    def tap(a, j, h):
        return taps_ref[a, pl.ds(j, 1), columns(h)]

    def filtered(wide, taps_here, at):
        value = taps_here[0] * wide[pl.ds(RIM + at, chunk), :]
        for j in range(1, 3):
            value = value + taps_here[j] * wide[pl.ds(RIM + at - j, chunk), :]
        return value.astype(BF16)

    def featurize_own(h, carry):
        for a, target in enumerate((qfb.at[h], kfb.at[h], vfb.at[h])):
            base = 0 if a == 0 else past
            taps_here = [tap(a, j, h) for j in range(3)]
            wide = wide_own.at[h, a]
            wide[pl.ds(0, RIM), :] = near_rim[a, :, columns(h)].astype(F32)
            for i in range(rows // chunk):
                wide[pl.ds(RIM + i * chunk, chunk), :] = held[
                    a, pl.ds(i * chunk, chunk), columns(h)
                ].astype(F32)
                target[pl.ds(base + i * chunk, chunk), :] = filtered(wide, taps_here, i * chunk)
        return carry

    load(1).wait()
    load(2).wait()
    send_step(0, 0)
    load(0).wait()
    rim_out[...] = held[pl.ds(0, 3), pl.ds(rows - RIM, RIM), :]
    to_next.start()
    to_far.start()
    total[...] = jnp.zeros_like(total)
    for i in range(2):
        if width_of(i) < nkeys:
            blank = (pl.ds(i * tile, tile), pl.ds(width_of(i), nkeys - width_of(i)))
            for buf in (pbuf, dsbuf):
                buf[blank] = jnp.zeros((tile, nkeys - width_of(i)), BF16)
    send_step(1, 0)
    to_next.wait_recv()
    to_far.wait_recv()
    load(3).wait()
    lax.fori_loop(0, heads, featurize_own, 0)
    send_step(2, 0)
    if heads > 1:
        send_step(0, 1)

    def pass_back(step, h, a):
        return pltpu.make_async_remote_copy(
            src_ref=term_out.at[h, step, a],
            dst_ref=term_in.at[h, step, a],
            send_sem=bwd_send.at[step, h, a],
            recv_sem=bwd_recv.at[step, h, a],
            device_id=behind,
            device_id_type=MESH,
        )

    def send_back(step, h):
        for a in range(2):
            if step > 0:
                pass_back(step - 1, h, a).wait_recv()

            def piece(i, carry):
                at = pl.multiple_of(i * chunk, 16)
                here = pl.ds(at, chunk)
                term = dkv[h, a, pl.ds(step * rows + at, chunk), :]
                if step > 0:
                    term = term + decode(term_in[h, step - 1, a, here, :])
                term_out[h, step, a, here, :] = encode(term)
                return carry

            lax.fori_loop(0, rows // chunk, piece, 0)
            pass_back(step, h, a).start()

    def tail(h):
        return pltpu.make_async_remote_copy(
            src_ref=tail_out.at[h],
            dst_ref=tail_in.at[h],
            send_sem=tail_send.at[h],
            recv_sem=tail_recv.at[h],
            device_id=behind,
            device_id_type=MESH,
        )

    def settle(h, with_taps):
        last = STEPS - 1

        for a in range(2):
            pass_back(last, h, a).wait_recv()

        def piece(i, carry):
            at = pl.multiple_of(i * chunk, 16)
            here = pl.ds(at, chunk)
            dext[0, here, :] = dqb[h, here, :].astype(F32)
            for a in range(2):
                own = dkv[h, a, pl.ds(past + at, chunk), :]
                total_here = own + decode(term_in[h, last, a, here, :])
                dext[a + 1, here, :] = total_here.astype(BF16).astype(F32)
            return carry

        lax.fori_loop(0, rows // chunk, piece, 0)
        for a in range(3):
            tail_out[h, a] = dext[a, pl.ds(0, RIM), :].astype(BF16)
        tail(h).start()
        if with_taps:
            for a in range(3):
                tap_sums(h, a, wide_own.at[h, a], lambda at, n=a: dext[n, pl.ds(at, chunk), :])

    def tap_sums(h, a, wide, gradient):
        sums = [jnp.zeros((8, HEAD_DIM), F32) for _ in range(3)]
        for i in range(rows // chunk):
            value = gradient(i * chunk)
            for j in range(3):
                near = wide[pl.ds(RIM - j + i * chunk, chunk), :]
                sums[j] = sums[j] + jnp.sum((value * near).reshape(chunk // 8, 8, HEAD_DIM), axis=0)
        for j in range(3):
            here = pl.ds(3 * a + j, 1)
            total[h, here, :] = total[h, here, :] + jnp.sum(sums[j], axis=0, keepdims=True)

    def finish(h):
        tail(h).wait_recv()
        for a in range(3):
            dext[a, pl.ds(rows, RIM), :] = tail_in[h, a].astype(F32)
            taps_here = [tap(a, j, h) for j in range(3)]
            for i in range(rows // chunk):
                value = jnp.zeros((chunk, HEAD_DIM), F32)
                for j in range(3):
                    value = value + taps_here[j] * dext[a, pl.ds(i * chunk + j, chunk), :]
                (gq_ref, gk_ref, gv_ref)[a][pl.ds(i * chunk, chunk), columns(h)] = value.astype(BF16)

    def featurize(h):
        for a, target in enumerate((kfb.at[h], vfb.at[h])):
            taps_here = [tap(a + 1, j, h) for j in range(3)]
            wide = ext.at[a]
            wide[pl.ds(0, RIM), :] = far_rim[a, :, columns(h)].astype(F32)
            for i in range(past // chunk):
                here = pl.ds(i * chunk, chunk)
                wide[pl.ds(RIM + i * chunk, chunk), :] = raw[h, a, here, :].astype(F32)
                target[pl.ds(i * chunk, chunk), :] = filtered(wide, taps_here, i * chunk)

    def products(h, i):
        here = pl.ds(i * tile, tile)
        q = qfb[h, here, :]
        g = held[3, here, columns(h)]
        peak = None
        for start in range(0, width_of(i), 256):
            size = min(256, width_of(i) - start)
            part = pl.ds(start, size)
            score = dot(q, kfb[h, part, :], NT)
            if start + size > past + i * tile:
                row = lax.broadcasted_iota(jnp.int32, score.shape, 0) + i * tile
                col = lax.broadcasted_iota(jnp.int32, score.shape, 1) + (start - past)
                score = jnp.where(col <= row, score, -jnp.inf)
            sbuf[i, :, part] = score
            for n in range(0, size, HEAD_DIM):
                piece = score[:, n : n + HEAD_DIM]
                peak = piece if peak is None else jnp.maximum(peak, piece)
            dpbuf[i, :, part] = dot(g, vfb[h, part, :], NT)
        return jnp.max(peak, axis=1, keepdims=True)

    def weigh(i, peak):
        cols = pl.ds(0, width_of(i))
        stats = []
        for r in range(0, tile, strip):
            here = pl.ds(r, strip)
            weight = jnp.exp2((sbuf[i, here, cols] - peak[r : r + strip]) * exp_scale)
            sbuf[i, here, cols] = weight
            inverse = 1.0 / jnp.sum(weight, axis=1, keepdims=True)
            delta = jnp.sum(weight * dpbuf[i, here, cols], axis=1, keepdims=True) * inverse
            stats.append((inverse, delta))
        return stats

    def settle_scores(i, stats):
        cols = pl.ds(0, width_of(i))
        for n, (inverse, delta) in enumerate(stats):
            here = pl.ds(n * strip, strip)
            there = pl.ds(i * tile + n * strip, strip)
            prob = sbuf[i, here, cols] * inverse
            pbuf[there, cols] = prob.astype(BF16)
            dsbuf[there, cols] = (prob * (dpbuf[i, here, cols] - delta)).astype(BF16)

    def row_results(h, i):
        here = pl.ds(i * tile, tile)
        cols = pl.ds(0, width_of(i))
        out_ref[here, columns(h)] = dot(pbuf[here, cols], vfb[h, cols, :], NN).astype(BF16)
        dqb[h, here, :] = (dot(dsbuf[here, cols], kfb[h, cols, :], NN) * scale).astype(BF16)

    def attend_first(h):
        peak = products(h, 0)
        stats = weigh(0, peak)
        peak_next = products(h, 1)
        settle_scores(0, stats)
        stats_next = weigh(1, peak_next)
        for n, (inverse, delta) in enumerate(stats_next):
            here = pl.ds(n * strip, strip)
            norms[0, here, :] = jnp.broadcast_to(inverse, (strip, HEAD_DIM))
            norms[1, here, :] = jnp.broadcast_to(delta, (strip, HEAD_DIM))

    def attend_second(h):
        row_results(h, 0)
        stats = [
            (norms[0, pl.ds(r, strip), pl.ds(0, 1)], norms[1, pl.ds(r, strip), pl.ds(0, 1)])
            for r in range(0, tile, strip)
        ]
        settle_scores(1, stats)
        dkv[h, 1] = dot(held[3, :, columns(h)], pbuf[...], TN).T
        dkv[h, 0] = (dot(qfb[h], dsbuf[...], TN) * scale).T
        row_results(h, 1)

    def last_taps(h):
        tap_sums(h, 0, wide_own.at[h, 0], lambda at: dqb[h, pl.ds(at, chunk), :].astype(F32))
        for a in range(2):
            for block in range(BLOCKS):
                wide = wide_own.at[h, a + 1] if block == STEPS else ext.at[a, pl.ds(block * rows, RIM + rows), :]
                tap_sums(
                    h, a + 1, wide, lambda at, n=a, b=block: dkv[h, n, pl.ds(b * rows + at, chunk), :]
                )

    def head_step(h, carry):
        for a in range(2):
            pass_on(STEPS - 1, h, a).wait_recv()
        featurize(h)

        @pl.when(h < heads - 1)
        def _():
            send_step(1, h + 1)

        @pl.when(h > 1)
        def _():
            settle(h - 2, True)

        @pl.when(h > 0)
        def _():
            send_back(1, h - 1)

        attend_first(h)

        @pl.when(h < heads - 1)
        def _():
            send_step(2, h + 1)

        @pl.when(h < heads - 2)
        def _():
            send_step(0, h + 2)

        @pl.when(h > 0)
        def _():
            send_back(2, h - 1)

        @pl.when(h > 1)
        def _():
            finish(h - 2)

        attend_second(h)

        send_back(0, h)
        return carry

    lax.fori_loop(0, heads, head_step, 0)

    def sum_copy(n, m):
        group = groups[n]
        slot, device = group.other(m)
        return slot, pltpu.make_async_remote_copy(
            src_ref=slots.at[n, group.index],
            dst_ref=slots.at[n, group.index],
            send_sem=sum_send.at[n, m],
            recv_sem=sum_recv.at[n, group.index],
            device_id=device,
            device_id_type=MESH,
        )

    def sum_start(n, value):
        slots[n, groups[n].index] = value
        for m in range(1, groups[n].size):
            sum_copy(n, m)[1].start()

    def sum_end(n):
        group = groups[n]
        for m in range(1, group.size):
            slot, _ = group.other(m)
            pltpu.make_async_remote_copy(
                src_ref=slots.at[n, slot],
                dst_ref=slots.at[n, slot],
                send_sem=sum_send.at[n, m],
                recv_sem=sum_recv.at[n, slot],
                device_id=ahead,
                device_id_type=MESH,
            ).wait_recv()
        value = slots[n, 0]
        for slot in range(1, group.size):
            value = value + slots[n, slot]
        return value

    done = 0

    def sum_step():
        nonlocal done
        if done < len(groups) - 1:
            sum_start(done + 1, sum_end(done))
            done += 1

    last_taps(heads - 1)
    if heads > 1:
        settle(heads - 2, True)
    sum_start(0, total[...])
    send_back(1, heads - 1)
    if heads > 1:
        finish(heads - 2)
    sum_step()
    send_back(2, heads - 1)
    sum_step()
    settle(heads - 1, False)
    sum_step()
    finish(heads - 1)
    while done < len(groups) - 1:
        sum_step()
    value = sum_end(done)
    for h in range(heads):
        for a in range(3):
            gt_ref[a, :, columns(h)] = value[h, 3 * a : 3 * a + 3, :]

    for h in range(heads):
        tail(h).wait_send()
        for step in range(STEPS):
            for a in range(2):
                pass_on(step, h, a).wait_send()
                pass_back(step, h, a).wait_send()

    to_next.wait_send()
    to_far.wait_send()
    for n, group in enumerate(groups):
        for m in range(1, group.size):
            sum_copy(n, m)[1].wait_send()


def deliver(*refs):
    count = len(refs) // 2
    sources, targets, sems = refs[:count], refs[count : 2 * count], refs[-1]
    copies = [
        pltpu.make_async_copy(source, target, sems.at[n])
        for n, (source, target) in enumerate(zip(sources, targets, strict=True))
    ]
    for copy in copies:
        copy.start()
    for copy in copies:
        copy.wait()


def shards(n_dp, n_ctx, query_input, key_input, value_input, taps, grad_out):
    rows, width = query_input.shape[1:]
    heads = width // HEAD_DIM
    nkeys = BLOCKS * rows
    rounds = len(reduction_rounds(n_dp, n_ctx))
    members = 4 if (n_dp, n_ctx) == (8, 32) else max(n_dp, n_ctx)
    hbm = pl.BlockSpec(memory_space=pl.ANY)
    vmem = pl.BlockSpec(memory_space=pltpu.VMEM)
    flat = pltpu.VMEM((rows, width), BF16)
    dma = pltpu.SemaphoreType.DMA
    block = (rows, HEAD_DIM)
    results = pl.pallas_call(
        functools.partial(kernel, (rows, heads, n_dp, n_ctx)),
        out_shape=(flat, flat, flat, flat, pltpu.VMEM(taps.shape, F32)),
        in_specs=[hbm, hbm, hbm, vmem, hbm],
        out_specs=(vmem,) * 5,
        scratch_shapes=[
            pltpu.VMEM((4, rows, width), BF16),
            pltpu.VMEM((heads, 2, *block), BF16),
            pltpu.VMEM((3, RIM, width), BF16),
            pltpu.VMEM((3, RIM, width), BF16),
            pltpu.VMEM((2, RIM, width), BF16),
            pltpu.VMEM((heads, 2, STEPS * rows, HEAD_DIM), BF16),
            pltpu.VMEM((heads, 3, RIM + rows, HEAD_DIM), F32),
            pltpu.VMEM((2, RIM + STEPS * rows, HEAD_DIM), F32),
            pltpu.VMEM((2, rows // 2, HEAD_DIM), F32),
            pltpu.VMEM((heads, nkeys, HEAD_DIM), BF16),
            pltpu.VMEM((heads, nkeys, HEAD_DIM), BF16),
            pltpu.VMEM((heads, *block), BF16),
            pltpu.VMEM((2, rows // 2, nkeys), F32),
            pltpu.VMEM((2, rows // 2, nkeys), F32),
            pltpu.VMEM((rows, nkeys), BF16),
            pltpu.VMEM((rows, nkeys), BF16),
            pltpu.VMEM((heads, 2, nkeys, HEAD_DIM), F32),
            pltpu.VMEM((heads, *block), BF16),
            pltpu.VMEM((heads, STEPS, 2, *block), BF16),
            pltpu.VMEM((heads, STEPS, 2, *block), BF16),
            pltpu.VMEM((heads, 3, RIM, HEAD_DIM), BF16),
            pltpu.VMEM((heads, 3, RIM, HEAD_DIM), BF16),
            pltpu.VMEM((3, rows + RIM, HEAD_DIM), F32),
            pltpu.VMEM((heads, 16, HEAD_DIM), F32),
            pltpu.VMEM((rounds, members, heads, 16, HEAD_DIM), F32),
            dma((4,)),
            dma((2,)),
            dma((2,)),
            dma((STEPS, heads, 2)),
            dma((STEPS, heads, 2)),
            dma((STEPS, heads, 2)),
            dma((STEPS, heads, 2)),
            dma((heads,)),
            dma((heads,)),
            dma((rounds, members)),
            dma((rounds, members)),
        ],
        compiler_params=pltpu.CompilerParams(
            collective_id=0, has_side_effects=True, vmem_limit_bytes=52 * 1024 * 1024
        ),
    )(query_input[0], key_input[0], value_input[0], taps, grad_out[0])
    results = [pltpu.with_memory_space_constraint(result, pltpu.VMEM) for result in results]
    results = pl.pallas_call(
        deliver,
        out_shape=tuple(jax.ShapeDtypeStruct(result.shape, result.dtype) for result in results),
        in_specs=[vmem] * len(results),
        out_specs=(hbm,) * len(results),
        scratch_shapes=[dma((len(results),))],
    )(*results)
    return (*[result[None] for result in results[:4]], results[4])


def solution(mesh):
    sharded = P("dp", "ctx", "mp")
    return jax.shard_map(
        functools.partial(shards, mesh.shape["dp"], mesh.shape["ctx"]),
        mesh=mesh,
        in_specs=(sharded, sharded, sharded, P(None, None, "mp"), sharded),
        out_specs=(sharded, sharded, sharded, sharded, P(None, None, "mp")),
        check_vma=False,
    )
```

time: 96.9 us -> 88.4 us (0.912)
  the two profiles are of different devices: /device:TPU:32 before, /device:TPU:4 now
where the time goes in v2:
time: 88.4 us; the launch traced here: 88.3 us
  Pallas kernels  86.9 us (98%)
    pallas_call x1, Pallas kernels, shards(): pl.pallas_call(functools.partial(kernel, (rows, heads, n_dp, n_ctx)), out...  85.6 us

profile of v2, /device:TPU:4, one launch (start us, length us, event | category | flops | bytes accessed | tf_op | source)
XLA Modules:
  0.0 88.3 jit_solution(661516959869028520)
XLA Ops:
  0.6 0.0 copy-start
  0.6 0.7 copy-done
  1.4 85.6 %shard_map.92 = (bf16[448,512]{1,0:T(8,128)(2,1)S(1)}, bf16[448,512]{1,0:T(8,128)(2,1)S(1)}, bf16[448,512]{1,0:T(8,128)(2,1)S(1)}, bf16[448,512]{1,0:T(8,128)(2,1)S(1)}, f32[3,3,512]{2,1,0:T(4,128)S(1)}) custom-call(bf16[448,512]{1,0:T(8,128)(2,1)} %bitcast.8, bf16[448,512]{1,0:T(8,128)(2,1)} %bitcast.9, bf16[448,512]{1,0:T(8,128)(2,1)} %bitcast.10, ...), custom_call_target="tpu_custom_call" | custom-call | tf_op jit(solution)/shard_map/pallas_call | solution.py:516
  87.0 1.3 %shard_map.93 = (bf16[448,512]{1,0:T(8,128)(2,1)}, bf16[448,512]{1,0:T(8,128)(2,1)}, bf16[448,512]{1,0:T(8,128)(2,1)}, bf16[448,512]{1,0:T(8,128)(2,1)}, f32[3,3,512]{2,1,0:T(4,128)}) custom-call(bf16[448,512]{1,0:T(8,128)(2,1)S(1)} %get-tuple-element.15.refs_0_, bf16[448,512]{1,0:T(8,128)(2,1)S(1)} %get-tuple-element.16.refs_1_, ...), custom_call_target="tpu_custom_call" | custom-call | tf_op jit(solution)/shard_map/pallas_call | solution.py:564
Async XLA Ops:
  0.6 0.7 copy-start
